TPU v7x, 32 devices: a whole 2x2x4 slice. The times are simulated.
32 devices in a mesh: sector: 8 (over z, x), band: 4 (over y, core).
Axes of the slice: x: 2, y: 2, z: 4, core: 2. Of those that a mesh axis runs over, the one named last changes fastest.
Arguments:
- orbitals: bfloat16 [8, 32, 16, 4096], P('sector', None, None, 'band'), may hold values from -216 to 216
- potential: float32 [8, 32, 16], P('sector'), may hold values from 0.1 to 3
- near_points: int32 [128, 48], P('sector'), may hold values from 0 to 511
- near_values: bfloat16 [128, 48], P('sector'), may hold values from -0.875 to 0.875
- far_points: int32 [128, 16], P('sector'), may hold values from 0 to 511
- far_values: bfloat16 [128, 16], P('sector'), may hold values from -1.5 to 1.5
- atom_energy: float32 [128], P('sector'), may hold values from -1 to 2
Outputs:
- ham_panel: float32 [2048, 4096], P('sector', 'band')
- gram_panel: float32 [2048, 4096], P('sector', 'band')
Inputs may be any that keep to these rules, and one draw needn't show every extreme that they name: `near_points`: indices of points of the owning slab. `far_points`: row block s names points of slab s's first plane, for the atoms owned by slab s - 1 (mod 8).
All inputs are finite; a program needn't handle non-finite values.
Results may differ from a plain program's by a relative error of at most 0.00039.
Values may be sent and summed in bfloat16 or wider, within the bound.
A program may use at most 64 MiB of HBM per device.

v0:
```python
import jax
import jax.numpy as jnp
from jax import lax
from jax.sharding import PartitionSpec as P

TWIST = 3
PANEL = 2048


CENTER = 6.0
HALF_SPAN = 3.0


def padded_2(cells, sides, width):
    for axis, dim in sides:
        count = lax.axis_size(axis)
        head = lax.slice_in_dim(cells, 0, width, axis=dim)
        tail = lax.slice_in_dim(cells, cells.shape[dim] - width, cells.shape[dim], axis=dim)
        cells = jnp.concatenate(
            [
                lax.ppermute(tail, axis, [(i, (i + 1) % count) for i in range(count)]),
                cells,
                lax.ppermute(head, axis, [((i + 1) % count, i) for i in range(count)]),
            ],
            axis=dim,
        )
    return cells


def from_behind(array, axis, by):
    length = lax.axis_size(axis)
    return lax.ppermute(array, axis, [(i, (i + by) % length) for i in range(length)])


def build_dense(points, values, width):
    column_ids = jnp.arange(width, dtype=jnp.int32)
    matches = (points[:, :, None] == column_ids[None, None, :]).astype(jnp.float32)
    return jnp.sum(matches * values.astype(jnp.float32)[:, :, None], axis=1).astype(jnp.bfloat16)


def on_device(orbitals, potential, near_points, near_values, far_points, far_values, atom_energy):
    planes_dev, radial_cells, axial_cells, orb_count = orbitals.shape
    plane_size = radial_cells * axial_cells
    point_count = planes_dev * plane_size
    sector_pos = lax.axis_index("sector")
    sector_count = lax.axis_size("sector")
    near_dense = build_dense(near_points, near_values, point_count)
    far_dense = build_dense(far_points, far_values, plane_size)
    near_f = near_dense.astype(jnp.float32)
    far_f = far_dense.astype(jnp.float32)
    radius = (radial_cells + jnp.arange(radial_cells, dtype=jnp.float32))[None, :, None, None]
    weight = (radial_cells / radius) ** 2

    def operate(field_in):
        padded = padded_2(field_in, (("sector", 0),), 1)
        lower_plane = jnp.where(
            sector_pos == 0, jnp.roll(padded[0], TWIST, axis=1), padded[0]
        ).astype(jnp.float32)
        upper_plane = jnp.where(
            sector_pos == sector_count - 1, jnp.roll(padded[-1], -TWIST, axis=1), padded[-1]
        ).astype(jnp.float32)
        wavefunc = field_in.astype(jnp.float32)
        angular = (
            jnp.concatenate([wavefunc[1:], upper_plane[None]], 0)
            + jnp.concatenate([lower_plane[None], wavefunc[:-1]], 0)
            - 2.0 * wavefunc
        )
        zero_rim = jnp.zeros_like(wavefunc[:, :1])
        outer_rad = jnp.concatenate([wavefunc[:, 1:], zero_rim], 1)
        inner_rad = jnp.concatenate([zero_rim, wavefunc[:, :-1]], 1)
        radial = outer_rad + inner_rad - 2.0 * wavefunc + (outer_rad - inner_rad) / (2.0 * radius)
        axial_sum = jnp.roll(wavefunc, 1, axis=2) + jnp.roll(wavefunc, -1, axis=2) - 2.0 * wavefunc
        kinetic = -0.5 * (radial + axial_sum + weight * angular)
        flat_field = field_in.reshape(point_count, orb_count)
        near_coef = jnp.dot(near_dense, flat_field, preferred_element_type=jnp.float32)
        far_part = jnp.dot(
            far_dense,
            field_in[0].reshape(plane_size, orb_count),
            preferred_element_type=jnp.float32,
        )
        coeffs = near_coef + from_behind(far_part, "sector", -1)
        scaled = atom_energy[:, None] * coeffs
        before = from_behind(scaled, "sector", 1)
        spread = jnp.dot(near_f.T, scaled, precision=lax.Precision.HIGHEST).reshape(
            planes_dev, plane_size, orb_count
        )
        back_add = jnp.dot(far_f.T, before, precision=lax.Precision.HIGHEST)
        spread = (
            spread.at[0].add(back_add).reshape(planes_dev, radial_cells, axial_cells, orb_count)
        )
        return kinetic + potential[..., None] * wavefunc + spread

    orbitals32 = orbitals.astype(jnp.float32)
    first = ((operate(orbitals) - CENTER * orbitals32) / HALF_SPAN).astype(jnp.bfloat16)
    filtered = (
        2.0 * (operate(first) - CENTER * first.astype(jnp.float32)) / HALF_SPAN - orbitals32
    ).astype(jnp.bfloat16)
    image = operate(filtered).astype(jnp.bfloat16)
    filtered_flat = filtered.reshape(point_count, orb_count)
    image_flat = image.reshape(point_count, orb_count)
    panel_dev = PANEL // lax.axis_size("band")
    panel = lax.all_gather(filtered_flat[:, :panel_dev], "band", axis=1, tiled=True)
    grid_total = point_count * sector_count
    contract = (((0,), (0,)), ((), ()))
    columns = panel
    ham_panel = (
        lax.psum_scatter(
            lax.dot_general(columns, image_flat, contract, preferred_element_type=jnp.float32),
            "sector",
            scatter_dimension=0,
            tiled=True,
        )
        / grid_total
    )
    columns = panel
    gram_panel = (
        lax.psum_scatter(
            lax.dot_general(columns, filtered_flat, contract, preferred_element_type=jnp.float32),
            "sector",
            scatter_dimension=0,
            tiled=True,
        )
        / grid_total
    )
    return (ham_panel, gram_panel)


def solution(mesh):
    return jax.shard_map(
        on_device,
        mesh=mesh,
        in_specs=(
            P("sector", None, None, "band"),
            P("sector", None, None),
            P("sector", None),
            P("sector", None),
            P("sector", None),
            P("sector", None),
            P("sector"),
        ),
        out_specs=(P("sector", "band"), P("sector", "band")),
        check_vma=False,
    )
```

profile of v0, /device:TPU:0, one launch (start us, length us, event | category | flops | bytes accessed | tf_op | source)
XLA Modules:
  0.0 516.2 jit_solution(16188026082404697647)
XLA Ops:
  7.2 6.0 %collective-permute-start = (bf16[1,32,16,1024]{3,2,1,0:T(8,128)(2,1)}, bf16[1,32,16,1024]{3,2,1,0:T(8,128)(2,1)S(1)}, u32[]{:S(2)}, u32[]{:S(2)}) collective-permute-start(bf16[1,32,16,1024]{3,2,1,0:T(8,128)(2,1)} %param.13), channel_id=1, source_target_pairs={{4,0},{8,4},{12,8},{16,12},{20,16},{24,20},{28,24},{0,28},{5,1},{9... | collective-permute-start | bytes 3145736 | tf_op jit(solution)/shard_map/ppermute | solution.py:23
  13.3 0.7 convert_element_type.65
  13.9 0.9 select_reduce_fusion.1
  14.9 2.1 fusion.42
  17.0 4.7 collective-permute-start.2
  21.7 1.4 fusion.41
  23.1 2.5 fusion.39
  25.6 2.5 fusion.40
  28.1 0.4 select_reduce_fusion
  28.6 28.8 %collective-permute-done.2 = f32[16,1024]{1,0:T(8,128)S(1)} collective-permute-done((f32[16,1024]{1,0:T(8,128)}, f32[16,1024]{1,0:T(8,128)S(1)}, u32[]{:S(2)}, u32[]{:S(2)}) %collective-permute-start.2) | collective-permute-done | bytes 65568 | tf_op jit(solution)/shard_map/ppermute | solution.py:32
  57.7 6.9 %collective-permute-done.3 = f32[16,1024]{1,0:T(8,128)S(1)} collective-permute-done((f32[16,1024]{1,0:T(8,128)S(1)}, f32[16,1024]{1,0:T(8,128)S(1)}, u32[]{:S(2)}, u32[]{:S(2)}) %collective-permute-start.3) | collective-permute-done | bytes 65568 | tf_op jit(solution)/shard_map/ppermute | solution.py:32
  64.7 1.0 fusion.43
  65.7 1.1 convolution_add_fusion.2
  66.9 0.3 slice_bitcast_fusion.5
  67.5 0.4 copy-done.5
  67.9 0.9 copy-done.1
  68.8 0.6 copy-done.2
  69.4 3.6 fusion.8
  73.0 4.7 collective-permute-start.4
  77.7 0.5 fusion.37
  78.5 0.5 fusion.36
  79.0 41.1 %collective-permute-done.6 = f32[16,1024]{1,0:T(8,128)S(1)} collective-permute-done((f32[16,1024]{1,0:T(8,128)S(1)}, f32[16,1024]{1,0:T(8,128)S(1)}, u32[]{:S(2)}, u32[]{:S(2)}) %collective-permute-start.6) | collective-permute-done | bytes 65568 | tf_op jit(solution)/shard_map/ppermute | solution.py:32
  120.8 6.8 %collective-permute-done.7 = f32[16,1024]{1,0:T(8,128)S(1)} collective-permute-done((f32[16,1024]{1,0:T(8,128)S(1)}, f32[16,1024]{1,0:T(8,128)S(1)}, u32[]{:S(2)}, u32[]{:S(2)}) %collective-permute-start.7) | collective-permute-done | bytes 65568 | tf_op jit(solution)/shard_map/ppermute | solution.py:32
  127.5 1.0 fusion.45
  128.5 1.1 convolution_add_fusion.1
  130.0 0.3 slice_bitcast_fusion.3
  130.3 3.6 fusion.18
  134.2 0.8 slice.209
  135.0 4.7 collective-permute-start.8
  139.8 1.9 fusion.34
  141.7 0.5 fusion.33
  142.2 38.8 %collective-permute-done.10 = f32[16,1024]{1,0:T(8,128)S(1)} collective-permute-done((f32[16,1024]{1,0:T(8,128)S(1)}, f32[16,1024]{1,0:T(8,128)S(1)}, u32[]{:S(2)}, u32[]{:S(2)}) %collective-permute-start.10) | collective-permute-done | bytes 65568 | tf_op jit(solution)/shard_map/ppermute | solution.py:32
  181.5 6.8 %collective-permute-done.11 = f32[16,1024]{1,0:T(8,128)S(1)} collective-permute-done((f32[16,1024]{1,0:T(8,128)S(1)}, f32[16,1024]{1,0:T(8,128)S(1)}, u32[]{:S(2)}, u32[]{:S(2)}) %collective-permute-start.11) | collective-permute-done | bytes 65568 | tf_op jit(solution)/shard_map/ppermute | solution.py:32
  188.2 1.0 fusion.47
  189.3 1.1 convolution_add_fusion
  190.3 1.2 slice_bitcast_fusion.6
  191.5 1.1 slice_bitcast_fusion.7
  192.7 1.4 slice_bitcast_fusion
  194.1 1.6 slice_bitcast_fusion.1
  195.7 5.1 fusion.25
  200.8 7.5 %fusion.48 = f32[2048,1024]{1,0:T(8,128)} fusion(bf16[512,2048]{1,0:T(8,128)(2,1)} %all-gather.2.cloned.1.call-done, bf16[512,1024]{1,0:T(8,128)(2,1)} %bitcast.85), kind=kOutput, calls=%fused_computation.86 | convolution fusion | flops 2147483648 | bytes 11534336 | tf_op jit(solution)/shard_map/dot_general | solution.py:108
  208.4 0.3 reduce-scatter.5.cloned.1.call-start
  208.7 1.3 copy-done.10
  209.9 5.9 %fusion.49 = f32[2048,1024]{1,0:T(8,128)} fusion(bf16[512,2048]{1,0:T(8,128)(2,1)S(1)} %copy-done.10, bf16[512,1024]{1,0:T(8,128)(2,1)S(1)} %bitcast.69), kind=kOutput, calls=%fused_computation.87 | convolution fusion | flops 2147483648 | bytes 11534336 | tf_op jit(solution)/shard_map/dot_general | solution.py:118
  215.9 139.4 %reduce-scatter.3.cloned.1.call-done = f32[256,1024]{1,0:T(8,128)} async-done(((f32[2048,1024]{1,0:T(8,128)}), f32[256,1024]{1,0:T(8,128)}) %reduce-scatter.3.cloned.1.call-update) | async-done | bytes 1048592 | tf_op jit(solution)/shard_map/reduce_scatter | solution.py:107
  355.3 2.3 broadcast_multiply_fusion.1
  357.6 149.8 %reduce-scatter.5.cloned.1.call-done = f32[256,1024]{1,0:T(8,128)} async-done(((f32[2048,1024]{1,0:T(8,128)}), f32[256,1024]{1,0:T(8,128)}) %reduce-scatter.5.cloned.1.call-update) | async-done | bytes 1048592 | tf_op jit(solution)/shard_map/reduce_scatter | solution.py:117
  507.3 2.3 broadcast_multiply_fusion
  (54 shorter events, 2.8 us)
Async XLA Ops:
  7.2 15.9 %copy-start = (bf16[1,32,16,1024]{3,2,1,0:T(8,128)(2,1)S(1)}, bf16[1,32,16,1024]{3,2,1,0:T(8,128)(2,1)}, u32[]{:S(2)}) copy-start(bf16[1,32,16,1024]{3,2,1,0:T(8,128)(2,1)} %param.13) | copy-start | bytes 3145732
  7.2 193.7 %all-gather.2.cloned.1.call-start = ((), (), s32[]{:S(2)}) async-start(), calls=%async_computation.2 | async-start | bytes 2621440 | tf_op jit(solution)/shard_map/all_gather | solution.py:102
  7.2 59.6 %collective-permute-start = (bf16[1,32,16,1024]{3,2,1,0:T(8,128)(2,1)}, bf16[1,32,16,1024]{3,2,1,0:T(8,128)(2,1)S(1)}, u32[]{:S(2)}, u32[]{:S(2)}) collective-permute-start(bf16[1,32,16,1024]{3,2,1,0:T(8,128)(2,1)} %param.13), channel_id=1, source_target_pairs={{4,0},{8,4},{12,8},{16,12},{20,16},{24,20},{28,24},{0,28},{5,1},{9... | collective-permute-start | bytes 3145736 | tf_op jit(solution)/shard_map/ppermute | solution.py:23
  13.2 54.0 %collective-permute-start.1 = (bf16[1,32,16,1024]{3,2,1,0:T(8,128)(2,1)}, bf16[1,32,16,1024]{3,2,1,0:T(8,128)(2,1)S(1)}, u32[]{:S(2)}, u32[]{:S(2)}) collective-permute-start(bf16[1,32,16,1024]{3,2,1,0:T(8,128)(2,1)} %param.13), channel_id=1, source_target_pairs={{0,4},{4,8},{8,12},{12,16},{16,20},{20,24},{24,28},{28,0},{1,5},{5... | collective-permute-start | bytes 3145736 | tf_op jit(solution)/shard_map/ppermute | solution.py:21
  17.0 40.5 %collective-permute-start.2 = (f32[16,1024]{1,0:T(8,128)}, f32[16,1024]{1,0:T(8,128)S(1)}, u32[]{:S(2)}, u32[]{:S(2)}) collective-permute-start(f32[16,1024]{1,0:T(8,128)} %fusion.42), channel_id=1, source_target_pairs={{0,28},{4,0},{8,4},{12,8},{16,12},{20,16},{24,20},{28,24},{1,29},{... | collective-permute-start | bytes 196616 | tf_op jit(solution)/shard_map/ppermute | solution.py:32
  25.6 2.6 copy-start.9
  25.6 2.6 copy-start.7
  25.6 3.0 copy-start.6
  25.6 31.9 %copy-start.8 = (f32[16]{0:T(128)S(1)}, f32[16]{0:T(128)}, u32[]{:S(2)}) copy-start(f32[16]{0:T(128)} %param.19) | copy-start | bytes 196
  57.7 7.0 %collective-permute-start.3 = (f32[16,1024]{1,0:T(8,128)S(1)}, f32[16,1024]{1,0:T(8,128)S(1)}, u32[]{:S(2)}, u32[]{:S(2)}) collective-permute-start(f32[16,1024]{1,0:T(8,128)S(1)} %fusion.31), channel_id=1, source_target_pairs={{0,4},{4,8},{8,12},{12,16},{16,20},{20,24},{24,28},{28,0},{1,5},{5... | collective-permute-start | bytes 196616 | tf_op jit(solution)/shard_map/ppermute | solution.py:32
  65.7 1.8 copy-start.4
  65.7 2.2 copy-start.5
  66.9 1.9 copy-start.1
  66.9 2.5 copy-start.2
  72.9 56.7 %collective-permute-start.5 = (bf16[1,32,16,1024]{3,2,1,0:T(8,128)(2,1)S(1)}, bf16[1,32,16,1024]{3,2,1,0:T(8,128)(2,1)S(1)}, u32[]{:S(2)}, u32[]{:S(2)}) collective-permute-start(bf16[1,32,16,1024]{3,2,1,0:T(8,128)(2,1)S(1)} %fusion.8), channel_id=1, source_target_pairs={{0,4},{4,8},{8,12},{12,16},{16,20},{20,24},{24,28},{28,0},{1,5},{5... | collective-permute-start | bytes 3145736 | tf_op jit(solution)/shard_map/ppermute | solution.py:21
  73.0 56.9 %collective-permute-start.4 = (bf16[1,32,16,1024]{3,2,1,0:T(8,128)(2,1)S(1)}, bf16[1,32,16,1024]{3,2,1,0:T(8,128)(2,1)S(1)}, u32[]{:S(2)}, u32[]{:S(2)}) collective-permute-start(bf16[1,32,16,1024]{3,2,1,0:T(8,128)(2,1)S(1)} %fusion.8), channel_id=1, source_target_pairs={{4,0},{8,4},{12,8},{16,12},{20,16},{24,20},{28,24},{0,28},{5,1},{9... | collective-permute-start | bytes 3145736 | tf_op jit(solution)/shard_map/ppermute | solution.py:23
  78.5 41.6 %collective-permute-start.6 = (f32[16,1024]{1,0:T(8,128)S(1)}, f32[16,1024]{1,0:T(8,128)S(1)}, u32[]{:S(2)}, u32[]{:S(2)}) collective-permute-start(f32[16,1024]{1,0:T(8,128)S(1)} %fusion.44), channel_id=1, source_target_pairs={{0,28},{4,0},{8,4},{12,8},{16,12},{20,16},{24,20},{28,24},{1,29},{... | collective-permute-start | bytes 196616 | tf_op jit(solution)/shard_map/ppermute | solution.py:32
  120.4 7.1 %collective-permute-start.7 = (f32[16,1024]{1,0:T(8,128)S(1)}, f32[16,1024]{1,0:T(8,128)S(1)}, u32[]{:S(2)}, u32[]{:S(2)}) collective-permute-start(f32[16,1024]{1,0:T(8,128)S(1)} %fusion.30), channel_id=1, source_target_pairs={{0,4},{4,8},{8,12},{12,16},{16,20},{20,24},{24,28},{28,0},{1,5},{5... | collective-permute-start | bytes 196616 | tf_op jit(solution)/shard_map/ppermute | solution.py:32
  135.0 55.3 %collective-permute-start.9 = (bf16[1,32,16,1024]{3,2,1,0:T(8,128)(2,1)S(1)}, bf16[1,32,16,1024]{3,2,1,0:T(8,128)(2,1)}, u32[]{:S(2)}, u32[]{:S(2)}) collective-permute-start(bf16[1,32,16,1024]{3,2,1,0:T(8,128)(2,1)S(1)} %fusion.18), channel_id=1, source_target_pairs={{0,4},{4,8},{8,12},{12,16},{16,20},{20,24},{24,28},{28,0},{1,5},{5... | collective-permute-start | bytes 3145736 | tf_op jit(solution)/shard_map/ppermute | solution.py:21
  135.0 56.5 %collective-permute-start.8 = (bf16[1,32,16,1024]{3,2,1,0:T(8,128)(2,1)S(1)}, bf16[1,32,16,1024]{3,2,1,0:T(8,128)(2,1)}, u32[]{:S(2)}, u32[]{:S(2)}) collective-permute-start(bf16[1,32,16,1024]{3,2,1,0:T(8,128)(2,1)S(1)} %fusion.18), channel_id=1, source_target_pairs={{4,0},{8,4},{12,8},{16,12},{20,16},{24,20},{28,24},{0,28},{5,1},{9... | collective-permute-start | bytes 3145736 | tf_op jit(solution)/shard_map/ppermute | solution.py:23
  141.6 39.4 %collective-permute-start.10 = (f32[16,1024]{1,0:T(8,128)S(1)}, f32[16,1024]{1,0:T(8,128)S(1)}, u32[]{:S(2)}, u32[]{:S(2)}) collective-permute-start(f32[16,1024]{1,0:T(8,128)S(1)} %fusion.46), channel_id=1, source_target_pairs={{0,28},{4,0},{8,4},{12,8},{16,12},{20,16},{24,20},{28,24},{1,29},{... | collective-permute-start | bytes 196616 | tf_op jit(solution)/shard_map/ppermute | solution.py:32
  141.7 213.6 %reduce-scatter.3.cloned.1.call-start = ((), (), s32[]{:S(2)}) async-start(), calls=%async_computation.3 | async-start | bytes 9437184 | tf_op jit(solution)/shard_map/reduce_scatter | solution.py:107
  181.3 7.0 %collective-permute-start.11 = (f32[16,1024]{1,0:T(8,128)S(1)}, f32[16,1024]{1,0:T(8,128)S(1)}, u32[]{:S(2)}, u32[]{:S(2)}) collective-permute-start(f32[16,1024]{1,0:T(8,128)S(1)} %fusion.29), channel_id=1, source_target_pairs={{0,4},{4,8},{8,12},{12,16},{16,20},{20,24},{24,28},{28,0},{1,5},{5... | collective-permute-start | bytes 196616 | tf_op jit(solution)/shard_map/ppermute | solution.py:32
  192.7 3.0 copy-start.3
  208.4 1.6 copy-start.10
  208.4 298.9 %reduce-scatter.5.cloned.1.call-start = ((), (), s32[]{:S(2)}) async-start(), calls=%async_computation.4 | async-start | bytes 9437184 | tf_op jit(solution)/shard_map/reduce_scatter | solution.py:117
Sparse Core Ops, SparseCore 0:
  141.8 21.2 all-gather.1
  208.5 146.7 reduce-scatter.2
  359.3 147.9 reduce-scatter.4
where the time goes:
time: 517 us; the launch traced here: 516 us
  waiting for transfers between devices  418 us (81%)
  matrix products  23 us (4%)
  local copies, waits for them, and re-layouts  20.9 us (4%)
  starting transfers between devices  20.8 us (4%)
  other arithmetic  19 us (4%)
  between operations  14.1 us (3%)
    reduce_scatter x1, waiting for transfers between devices, on_device(): lax.psum_scatter(lax.dot_general(columns, filtered_flat, contract, prefer...  150 us
    reduce_scatter x1, waiting for transfers between devices, on_device(): lax.psum_scatter(lax.dot_general(columns, image_flat, contract, preferred...  139 us
    ppermute x6, waiting for transfers between devices, from_behind(): lax.ppermute(array, axis, [(i, (i + by) % length) for i in range(length)])  129 us
    ppermute x3, starting transfers between devices, padded_2(): lax.ppermute(head, axis, [((i + 1) % count, i) for i in range(count)])  15.5 us
  transfers between devices with their start and end apart: 15, of which 8 were waited for; matrix products, arithmetic and copies ran while one was open for 8% of the time, Pallas kernels for 0%

commit v1 on v0

v1 whole, which is shorter than its diff:
```python
import functools

import jax
import jax.numpy as jnp
from jax import lax
from jax.experimental import pallas as pl
from jax.experimental.pallas import tpu as pltpu
from jax.sharding import PartitionSpec as P

MESH = pl.DeviceIdType.MESH
F32 = jnp.float32
BF16 = jnp.bfloat16

TWIST = 3
PANEL = 2048
CENTER = 6.0
HALF_SPAN = 3.0
LANES = 128
SKEW = 2


def build_dense(points, values, width):
    column_ids = jnp.arange(width, dtype=jnp.int32)
    matches = (points[:, :, None] == column_ids[None, None, :]).astype(F32)
    return jnp.sum(matches * values.astype(F32)[:, :, None], axis=1).astype(BF16)


def widen(tile, width):
    return jnp.concatenate([tile] * (width // LANES), axis=1) if width > LANES else tile


def kernel(n, nb, nr, nz, atoms, chunk, orb, bund, shifts, ham, gram,
           O, A, F, I, BB, W, G, D, CO, SP, ACC, PB, PT, PH, PG,
           send_sem, recv_sem, bsend_sem, brecv_sem, psend_sem, precv_sem):
    plane, cols = orb.shape
    rows = ham.shape[0]
    half = plane // 2
    chunks = cols // chunk
    steps = n // 2
    panel_dev = PANEL // nb
    pw = PB.shape[2]
    pieces = pw // LANES
    groups = panel_dev // pw
    order = [m * pieces + j for j in range(pieces) for m in range(groups)]
    order += list(range(panel_dev // LANES, cols // LANES))
    s = lax.axis_index("sector")
    b = lax.axis_index("band")

    def ring_sector(r):
        r = lax.rem(r + 2 * n, n)
        return jnp.where(r < n // 2, 2 * r, 2 * (n - 1 - r) + 1)

    pos = jnp.where(lax.rem(s, 2) == 0, s // 2, n - 1 - s // 2)
    ahead = ring_sector(pos + 1)
    behind = ring_sector(pos - 1)
    panel_row = s * rows
    owner = panel_row // panel_dev
    offset = panel_row - owner * panel_dev
    group = offset // pw
    sub = pl.multiple_of(offset - group * pw, 8)

    barrier = pltpu.get_barrier_semaphore()
    pl.semaphore_signal(barrier, inc=1, device_id={"sector": ahead}, device_id_type=MESH)
    pl.semaphore_signal(barrier, inc=1, device_id={"sector": behind}, device_id_type=MESH)
    for d in range(1, nb):
        pl.semaphore_signal(barrier, inc=1, device_id={"band": lax.rem(b + d, nb)}, device_id_type=MESH)

    for j, source in enumerate(order):
        O[s + 1, nz:nz + plane, j * LANES:(j + 1) * LANES] = orb[:, source * LANES:(source + 1) * LANES]
    BB[s] = bund[...]
    pl.semaphore_wait(barrier, 2 + nb - 1)

    def block_copy(c, k, way):
        blk = ring_sector(pos - k if way == 0 else pos + k)
        if k == steps - 1:
            span = pl.ds(nz + way * half, half)
        else:
            span = pl.ds(nz, plane)
        ref = O.at[blk + 1, span, pl.ds(c * chunk, chunk)]
        return pltpu.make_async_remote_copy(
            src_ref=ref, dst_ref=ref, send_sem=send_sem.at[way, c, k], recv_sem=recv_sem.at[way, c, k],
            device_id={"sector": ahead if way == 0 else behind}, device_id_type=MESH)

    def bundle_copy(k, way):
        blk = ring_sector(pos - k if way == 0 else pos + k)
        ref = BB.at[blk]
        return pltpu.make_async_remote_copy(
            src_ref=ref, dst_ref=ref, send_sem=bsend_sem.at[way, k], recv_sem=brecv_sem.at[way, k],
            device_id={"sector": ahead if way == 0 else behind}, device_id_type=MESH)

    def block_wait(c, k, way):
        blk = ring_sector(pos - k - 1 if way == 0 else pos + k + 1)
        if k == steps - 1:
            span = pl.ds(nz + way * half, half)
        else:
            span = pl.ds(nz, plane)
        ref = O.at[blk + 1, span, pl.ds(c * chunk, chunk)]
        pltpu.make_async_remote_copy(
            src_ref=ref, dst_ref=ref, send_sem=send_sem.at[way, c, k], recv_sem=recv_sem.at[way, c, k],
            device_id={"sector": ahead if way == 0 else behind}, device_id_type=MESH).wait_recv()

    def bundle_wait(k, way):
        blk = ring_sector(pos - k - 1 if way == 0 else pos + k + 1)
        ref = BB.at[blk]
        pltpu.make_async_remote_copy(
            src_ref=ref, dst_ref=ref, send_sem=bsend_sem.at[way, k], recv_sem=brecv_sem.at[way, k],
            device_id={"sector": ahead if way == 0 else behind}, device_id_type=MESH).wait_recv()

    def bundle_ways(k):
        return (0,) if k == steps - 1 else (0, 1)

    def panel_copy(j, d):
        lane = pl.multiple_of((j * groups + group) * LANES, LANES)
        return pltpu.make_async_remote_copy(
            src_ref=F.at[pl.ds(1, n), pl.ds(nz, plane), pl.ds(lane, LANES)],
            dst_ref=PB.at[:, :, pl.ds(j * LANES, LANES)],
            send_sem=psend_sem.at[j, d], recv_sem=precv_sem.at[j],
            device_id={"band": lax.rem(b + d, nb)}, device_id_type=MESH)

    for way in bundle_ways(0):
        bundle_copy(0, way).start()
    for c in range(min(2, chunks)):
        for way in (0, 1):
            block_copy(c, 0, way).start()

    for ref in (O, F):
        @pl.loop(0, n)
        def _(p):
            ref[p + 1, 0:nz, :] = jnp.zeros((nz, cols), BF16)
            ref[p + 1, nz + plane:nz + plane + nz, :] = jnp.zeros((nz, cols), BF16)

    @pl.loop(0, n)
    def _(p):
        A[p + 1, 0:nz, :] = jnp.zeros((nz, chunk), BF16)
        A[p + 1, nz + plane:nz + plane + nz, :] = jnp.zeros((nz, chunk), BF16)
        SP[p] = jnp.zeros(SP.shape[1:], BF16)

    def setup():
        @pl.loop(0, n)
        def _(p):
            dense = BB[p, 0:2 * atoms, :]
            W[p] = dense.astype(BF16)
            copies = LANES // (2 * atoms)
            G[p] = jnp.concatenate([dense] * copies, axis=0).T.astype(BF16)
            local = jnp.broadcast_to(BB[p, 3 * atoms:3 * atoms + 1, :], (LANES, plane)).T
            for i in range(nr):
                w = (nr / (nr + i)) ** 2
                D[p, i * nz:(i + 1) * nz, :] = local[i * nz:(i + 1) * nz] + (2.0 + w)

    def prepare(v, cs):
        for h in range(2):
            r = nz + h * half
            v[0, r:r + half, cs] = jnp.dot(shifts[1], v[n, r:r + half, cs], preferred_element_type=F32).astype(BF16)
            v[n + 1, r:r + half, cs] = jnp.dot(shifts[2], v[1, r:r + half, cs], preferred_element_type=F32).astype(BF16)

        @pl.loop(0, n)
        def _(p):
            CO[p] = jnp.dot(W[p], v[p + 1, nz:nz + plane, cs], preferred_element_type=F32)

        @pl.loop(0, n)
        def _(p):
            after = lax.rem(p + 1, n)
            energy = widen(BB[p, 2 * atoms:3 * atoms, 0:LANES], chunk)
            rest = energy * (CO[p, 0:atoms, :] + CO[after, atoms:2 * atoms, :])
            for term in range(3):
                part = rest.astype(BF16)
                rest = rest - part.astype(F32)
                r = term * 2 * atoms
                SP[p, r:r + atoms, :] = part
                SP[after, r + atoms:r + 2 * atoms, :] = part

    def operate(v, cs, finish):
        prepare(v, cs)

        @pl.loop(0, n)
        def _(p):
            for h in range(2):
                base = nz + h * half
                ACC[...] = (
                    jnp.dot(shifts[0], v[p + 1, base:base + half, cs], preferred_element_type=F32)
                    + jnp.dot(G[p, h * half:(h + 1) * half, :], SP[p], preferred_element_type=F32))
                for i in range(half // nz):
                    ri = nr + h * (half // nz) + i
                    r = base + i * nz
                    centre = v[p + 1, r:r + nz, cs].astype(F32)
                    outer = v[p + 1, r + nz:r + 2 * nz, cs].astype(F32)
                    inner = v[p + 1, r - nz:r, cs].astype(F32)
                    sides = v[p + 2, r:r + nz, cs].astype(F32) + v[p, r:r + nz, cs].astype(F32)
                    local = widen(D[p, r - nz:r, :], chunk)
                    value = (
                        ACC[i * nz:(i + 1) * nz, :]
                        + (-0.5 * (1.0 + 1.0 / (2.0 * ri))) * outer
                        + (-0.5 * (1.0 - 1.0 / (2.0 * ri))) * inner
                        + (-0.5 * (nr / ri) ** 2) * sides
                        + local * centre)
                    finish(p, r, centre, value)

    def stage_first(c):
        cs = slice(c * chunk, (c + 1) * chunk)

        def finish(p, r, centre, value):
            A[p + 1, r:r + nz, :] = ((value - CENTER * centre) * (1.0 / HALF_SPAN)).astype(BF16)

        operate_from(O, cs, finish)

    def operate_from(v, cs, finish):
        operate(v, cs, finish)

    def stage_filtered(c):
        cs = slice(c * chunk, (c + 1) * chunk)

        def finish(p, r, centre, value):
            start = O[p + 1, r:r + nz, cs].astype(F32)
            F[p + 1, r:r + nz, cs] = (
                (value - CENTER * centre) * (2.0 / HALF_SPAN) - start).astype(BF16)

        operate(A, slice(0, chunk), finish)

    def panel_send(j):
        @pl.when(b == owner)
        def _():
            for d in range(1, nb):
                panel_copy(j, d).start()
            lane = pl.multiple_of((j * groups + group) * LANES, LANES)

            @pl.loop(0, n)
            def _(p):
                PB[p, :, j * LANES:(j + 1) * LANES] = F[p + 1, nz:nz + plane, pl.ds(lane, LANES)]

    def stage_image(c):
        cs = slice(c * chunk, (c + 1) * chunk)

        def finish(p, r, centre, value):
            I[p, r - nz:r, cs] = value.astype(BF16)

        operate(F, cs, finish)

    def panel_ready():
        @pl.when(b != owner)
        def _():
            for j in range(pieces):
                panel_copy(j, 1).wait_recv()

        @pl.loop(0, n)
        def _(p):
            PT[p] = PB[p].T

    def project(c):
        cs = slice(c * chunk, (c + 1) * chunk)
        PG[...] = jnp.zeros(PG.shape, F32)
        PH[...] = jnp.zeros(PH.shape, F32)

        @pl.loop(0, n)
        def _(p):
            PG[...] += jnp.dot(PT[p], F[p + 1, nz:nz + plane, cs], preferred_element_type=F32)
            PH[...] += jnp.dot(PT[p], I[p, :, cs], preferred_element_type=F32)

        scale = 1.0 / (plane * n)
        for q in range(chunk // LANES):
            source = order[c * (chunk // LANES) + q]
            place = slice(source * LANES, (source + 1) * LANES)
            lanes = slice(q * LANES, (q + 1) * LANES)
            gram[:, place] = PG[pl.ds(sub, rows), lanes] * scale
            ham[:, place] = PH[pl.ds(sub, rows), lanes] * scale

    piece_chunk = [((j + 1) * groups * LANES - 1) // chunk for j in range(pieces)]
    work = {}
    last_slot = SKEW * (chunks - 1) + steps - 1
    for c in range(chunks):
        t = SKEW * c + steps - 1
        early, late = work.setdefault(t, []), work.setdefault(t + 1, [])
        if c == 0:
            early.append(setup)
        early.append(functools.partial(stage_first, c))
        early.append(functools.partial(stage_filtered, c))
        for j in range(pieces):
            if piece_chunk[j] == c:
                early.append(functools.partial(panel_send, j))
        late.append(functools.partial(stage_image, c))
    tail = []
    for t in range(last_slot + 1):
        if t < steps:
            for way in bundle_ways(t):
                bundle_wait(t, way)
            if t + 1 < steps:
                for way in bundle_ways(t + 1):
                    bundle_copy(t + 1, way).start()
        for c in range(chunks):
            k = t - SKEW * c
            if 0 <= k < steps:
                for way in (0, 1):
                    block_wait(c, k, way)
                    if k + 1 < steps:
                        block_copy(c, k + 1, way).start()
            if c >= 2 and t == SKEW * (c - 1) - 1:
                for way in (0, 1):
                    block_copy(c, 0, way).start()
        for item in work.get(t, []):
            item()
    for t in sorted(work):
        if t > last_slot:
            for item in work[t]:
                item()
    panel_ready()
    for c in range(chunks):
        project(c)

    for k in range(steps):
        for way in bundle_ways(k):
            bundle_copy(k, way).wait_send()
        for c in range(chunks):
            for way in (0, 1):
                block_copy(c, k, way).wait_send()

    @pl.when(b == owner)
    def _():
        for j in range(pieces):
            for d in range(1, nb):
                panel_copy(j, d).wait_send()


def shift_matrices(size, nz):
    row = jnp.arange(size)[:, None]
    col = jnp.arange(size)[None, :]
    same = row // nz == col // nz
    gap = (col - row) % nz
    near = jnp.where(same & ((gap == 1) | (gap == nz - 1)), -0.5, 0.0)
    lower = jnp.where(same & (gap == nz - TWIST), 1.0, 0.0)
    upper = jnp.where(same & (gap == TWIST), 1.0, 0.0)
    return jnp.stack([near, lower, upper]).astype(BF16)


def on_device(n, nb, orbitals, potential, near_points, near_values, far_points, far_values, atom_energy):
    _, nr, nz, cols = orbitals.shape
    plane = nr * nz
    atoms = near_points.shape[0]
    near = build_dense(near_points, near_values, plane).astype(F32)
    far = build_dense(far_points, far_values, plane).astype(F32)
    energy = jnp.broadcast_to(atom_energy[:, None], (atoms, plane))
    local = jnp.broadcast_to(potential.reshape(1, plane), (8, plane))
    bund = jnp.concatenate([near, far, energy, local], axis=0)
    shifts = shift_matrices(plane // 2, nz)
    chunk = 256 if cols >= 512 else LANES
    chunks = cols // chunk
    rows = PANEL // n
    pw = max(rows, LANES)
    pieces = pw // LANES
    steps = n // 2
    tall = plane + 2 * nz
    vmem = pl.BlockSpec(memory_space=pltpu.VMEM)
    return pl.pallas_call(
        functools.partial(kernel, n, nb, nr, nz, atoms, chunk),
        out_shape=(jax.ShapeDtypeStruct((rows, cols), F32),) * 2,
        in_specs=[vmem] * 3,
        out_specs=(vmem,) * 2,
        scratch_shapes=[
            pltpu.VMEM((n + 2, tall, cols), BF16),
            pltpu.VMEM((n + 2, tall, chunk), BF16),
            pltpu.VMEM((n + 2, tall, cols), BF16),
            pltpu.VMEM((n, plane, cols), BF16),
            pltpu.VMEM((n,) + bund.shape, F32),
            pltpu.VMEM((n, 2 * atoms, plane), BF16),
            pltpu.VMEM((n, plane, LANES), BF16),
            pltpu.VMEM((n, plane, LANES), F32),
            pltpu.VMEM((n, 2 * atoms, chunk), F32),
            pltpu.VMEM((n, LANES, chunk), BF16),
            pltpu.VMEM((plane // 2, chunk), F32),
            pltpu.VMEM((n, plane, pw), BF16),
            pltpu.VMEM((n, pw, plane), BF16),
            pltpu.VMEM((pw, chunk), F32),
            pltpu.VMEM((pw, chunk), F32),
            pltpu.SemaphoreType.DMA((2, chunks, steps)),
            pltpu.SemaphoreType.DMA((2, chunks, steps)),
            pltpu.SemaphoreType.DMA((2, steps)),
            pltpu.SemaphoreType.DMA((2, steps)),
            pltpu.SemaphoreType.DMA((pieces, nb)),
            pltpu.SemaphoreType.DMA((pieces,)),
        ],
        compiler_params=pltpu.CompilerParams(
            collective_id=0, has_side_effects=True, vmem_limit_bytes=60 * 2 ** 20
        ),
    )(orbitals.reshape(plane, cols), bund, shifts)


def solution(mesh):
    n, nb = mesh.shape["sector"], mesh.shape["band"]
    return jax.shard_map(
        functools.partial(on_device, n, nb),
        mesh=mesh,
        in_specs=(
            P("sector", None, None, "band"),
            P("sector", None, None),
            P("sector", None),
            P("sector", None),
            P("sector", None),
            P("sector", None),
            P("sector"),
        ),
        out_specs=(P("sector", "band"), P("sector", "band")),
        check_vma=False,
    )
```

time: 517 us -> 154 us (0.30)
  waiting for transfers between devices: 418 us -> 0 us
  Pallas kernels: 0 us -> 142 us
  matrix products: 23 us -> 0 us
  starting transfers between devices: 20.8 us -> 0 us
  local copies, waits for them, and re-layouts: 20.9 us -> 4.96 us
  other arithmetic: 19 us -> 5.2 us
  between operations: 14.1 us -> 0.68 us
    reduce_scatter x2 -> x0, waiting for transfers between devices: 289 us -> none  [the longest x1 150 us: on_device(): lax.psum_scatter(lax.dot_general(columns, filtered_flat, contract, prefer...]
    pallas_call x0 -> x1, Pallas kernels: none -> 142 us  [on_device(): pl.pallas_call(functools.partial(kernel, n, nb, nr, nz, atoms, chunk), ou...]
    ppermute x12 -> x0, waiting for transfers between devices: 129 us -> none  [the longest x6 129 us: from_behind(): lax.ppermute(array, axis, [(i, (i + by) % length) for i in range(length)])]
    dot_general x14 -> x0, matrix products: 23 us -> none  [the longest x1 7.51 us: on_device(): lax.dot_general(columns, image_flat, contract, preferred_element_type=jnp...]
    ppermute x12 -> x0, starting transfers between devices: 20.4 us -> none  [the longest x3 15.5 us: padded_2(): lax.ppermute(head, axis, [((i + 1) % count, i) for i in range(count)])]
    convert_element_type x5 -> x4, other arithmetic: 13 us -> 1.39 us  [the longest x2 1.38 us: build_dense(): values.astype(F32)[:, :, None]]
    slice x10 -> x0, local copies, waits for them, and re-layouts: 11 us -> none  [the longest x6 6.73 us: operate(): jnp.roll(wavefunc, -1, axis=2)]
    concatenate x12 -> x1, local copies, waits for them, and re-layouts: 6.6 us -> 0.73 us  [on_device(): bund = jnp.concatenate([near, far, energy, local], axis=0)]
  transfers between devices with their start and end apart: 15 -> 0, of which waited for: 8 -> 0; matrix products, arithmetic and copies ran while one was open for 8% -> 0% of each run, Pallas kernels for 0% -> 0%
where the time goes in v1:
time: 154 us; the launch traced here: 153 us
  Pallas kernels  142 us (92%)
  other arithmetic  5.2 us (3%)
  local copies, waits for them, and re-layouts  4.96 us (3%)
    pallas_call x1, Pallas kernels, on_device(): pl.pallas_call(functools.partial(kernel, n, nb, nr, nz, atoms, chunk), ou...  142 us
    unnamed x5, local copies, waits for them, and re-layouts  4.14 us

profile of v1, /device:TPU:0, one launch (start us, length us, event | category | flops | bytes accessed | tf_op | source)
XLA Modules:
  0.0 153.2 jit_solution(13558305561487518578)
XLA Ops:
  0.6 0.7 pad.5.clone
  1.4 0.7 convert_element_type.21
  2.1 1.1 select_reduce_fusion
  3.2 0.7 convert_element_type.24
  3.9 0.9 select_reduce_fusion.1
  4.8 0.8 copy.10
  5.6 0.1 broadcast_in_dim.36
  5.7 0.7 pad_maximum_fusion.1.bund
  6.4 0.3 select_convert_fusion.2
  6.7 0.8 pad_maximum_fusion.shifts
  7.5 142.4 %shard_map.86 = (f32[256,1024]{1,0:T(8,128)}, f32[256,1024]{1,0:T(8,128)}) custom-call(bf16[512,1024]{1,0:T(8,128)(2,1)} %bitcast.1, f32[56,512]{1,0:T(8,128)} %pad_maximum_fusion.1.bund, bf16[3,256,256]{2,1,0:T(8,128)(2,1)} %pad_maximum_fusion.shifts), custom_call_target="tpu_custom_call" | custom-call | tf_op jit(solution)/shard_map/pallas_call | solution.py:351
  149.9 0.0 copy-start
  149.9 2.4 %copy.13 = f32[256,1024]{1,0:T(8,128)} copy(f32[256,1024]{1,0:T(8,128)} %get-tuple-element.7) | data formatting | bytes 2097152
  152.3 0.0 copy-done
  152.3 1.0 copy.14
  (4 shorter events, 0.0 us)
Async XLA Ops:
  149.9 2.4 %copy-start = (f32[256,1024]{1,0:T(8,128)S(1)}, f32[256,1024]{1,0:T(8,128)}, u32[]{:S(2)}) copy-start(f32[256,1024]{1,0:T(8,128)} %get-tuple-element.8) | copy-start | bytes 3145732

commit v2 on v1

v2 whole, which is shorter than its diff:
```python
import functools

import jax
import jax.numpy as jnp
from jax import lax
from jax.experimental import pallas as pl
from jax.experimental.pallas import tpu as pltpu
from jax.sharding import PartitionSpec as P

MESH = pl.DeviceIdType.MESH
F32 = jnp.float32
BF16 = jnp.bfloat16

TWIST = 3
PANEL = 2048
CENTER = 6.0
HALF_SPAN = 3.0
LANES = 128
SKEW = 2


def build_dense(points, values, width):
    column_ids = jnp.arange(width, dtype=jnp.int32)
    matches = (points[:, :, None] == column_ids[None, None, :]).astype(F32)
    return jnp.sum(matches * values.astype(F32)[:, :, None], axis=1).astype(BF16)


def widen(tile, width):
    return jnp.concatenate([tile] * (width // LANES), axis=1) if width > LANES else tile


def kernel(n, nb, nr, nz, atoms, chunk, batch, orb, bund, shifts, ham, gram,
           O, A, F, I, BB, W, G, D, CO, SP, ACC, PB, PT, PH, PG, RH, RG,
           xs, xr, zs, zr, bxs, bxr, bzs, bzr, ps, pr, os, orr):
    plane, cols = orb.shape
    rows = ham.shape[0]
    half = plane // 2
    mine = cols // 2
    chunks = mine // chunk
    batches = mine // batch
    levels = n // 2
    panel_dev = PANEL // nb
    panel_blocks = panel_dev // LANES
    pieces = max(panel_blocks // 2, 1)
    both = panel_blocks >= 2
    order = list(range(pieces)) + ([panel_blocks + j for j in range(pieces)] if both else [])
    s = lax.axis_index("sector")
    b = lax.axis_index("band")
    x = lax.rem(s, 2)
    level = s // 2
    partner = s + 1 - 2 * x
    above, below = s + 2, s - 2
    core = lax.rem(b, 2)
    sibling = b + 1 - 2 * core
    owner = level

    def source_lane(j, side):
        return pl.multiple_of((order[j] + side * pieces) * LANES, LANES)

    def remote(src, dst, send, recv, **device):
        return pltpu.make_async_remote_copy(
            src_ref=src, dst_ref=dst, send_sem=send, recv_sem=recv, device_id=device, device_id_type=MESH)

    barrier = pltpu.get_barrier_semaphore()
    pl.semaphore_signal(barrier, inc=1, device_id={"sector": partner}, device_id_type=MESH)

    @pl.when(level < levels - 1)
    def _():
        pl.semaphore_signal(barrier, inc=1, device_id={"sector": above}, device_id_type=MESH)

    @pl.when(level > 0)
    def _():
        pl.semaphore_signal(barrier, inc=1, device_id={"sector": below}, device_id_type=MESH)

    for d in range(1, nb):
        pl.semaphore_signal(barrier, inc=1, device_id={"band": lax.rem(b + d, nb)}, device_id_type=MESH)

    for j in range(mine // LANES):
        O[s + 1, nz:nz + plane, j * LANES:(j + 1) * LANES] = orb[:, pl.ds(source_lane(j, x), LANES)]
    BB[s] = bund[...]
    ends = jnp.where(level == 0, 1, 0) + jnp.where(level == levels - 1, 1, 0)
    pl.semaphore_wait(barrier, nb + 2 - ends)

    per = chunk // LANES

    def cross(c):
        return remote(orb.at[:, pl.ds(source_lane(c * per, 1 - x), chunk)],
                      O.at[s + 1, pl.ds(nz, plane), pl.ds(c * chunk, chunk)],
                      xs.at[c], xr.at[c], sector=partner)

    def cross_wait(c):
        remote(orb.at[:, pl.ds(source_lane(c * per, x), chunk)],
               O.at[partner + 1, pl.ds(nz, plane), pl.ds(c * chunk, chunk)],
               xs.at[c], xr.at[c], sector=partner).wait_recv()

    def bundle_cross():
        return remote(BB.at[s], BB.at[s], bxs, bxr, sector=partner)

    def bundle_cross_wait():
        remote(BB.at[partner], BB.at[partner], bxs, bxr, sector=partner).wait_recv()

    def hop_parts(way, lv):
        if way == 0:
            return above
        return below

    def block_hop(c, lv, k, way):
        ref = O.at[pl.ds(2 * lv + 1, 2), pl.ds(nz, plane), pl.ds(c * chunk, chunk)]
        return remote(ref, ref, zs.at[way, c, k], zr.at[way, c, k], sector=hop_parts(way, lv))

    def bundle_hop(lv, k, way):
        ref = BB.at[pl.ds(2 * lv, 2)]
        return remote(ref, ref, bzs.at[way, k], bzr.at[way, k], sector=hop_parts(way, lv))

    def sends(make, k, act):
        @pl.when((level - k >= 0) & (level < levels - 1))
        def _():
            act(make(level - k, k, 0))

        @pl.when((level + k < levels) & (level > 0))
        def _():
            act(make(level + k, k, 1))

    def receives(make, k):
        @pl.when(level - 1 - k >= 0)
        def _():
            make(level - 1 - k, k, 0).wait_recv()

        @pl.when(level + 1 + k < levels)
        def _():
            make(level + 1 + k, k, 1).wait_recv()

    def chunk_hop(c):
        return functools.partial(block_hop, c)

    bundle_cross().start()
    for c in range(chunks):
        cross(c).start()

    for ref in (O, F):
        @pl.loop(0, n)
        def _(p):
            ref[p + 1, 0:nz, :] = jnp.zeros((nz, mine), BF16)
            ref[p + 1, nz + plane:nz + plane + nz, :] = jnp.zeros((nz, mine), BF16)

    @pl.loop(0, n)
    def _(p):
        A[p + 1, 0:nz, :] = jnp.zeros((nz, chunk), BF16)
        A[p + 1, nz + plane:nz + plane + nz, :] = jnp.zeros((nz, chunk), BF16)
        SP[p] = jnp.zeros(SP.shape[1:], BF16)

    def setup():
        @pl.loop(0, n)
        def _(p):
            dense = BB[p, 0:2 * atoms, :]
            W[p] = dense.astype(BF16)
            copies = LANES // (2 * atoms)
            G[p] = jnp.concatenate([dense] * copies, axis=0).T.astype(BF16)
            local = jnp.broadcast_to(BB[p, 3 * atoms:3 * atoms + 1, :], (LANES, plane)).T
            for i in range(nr):
                w = (nr / (nr + i)) ** 2
                D[p, i * nz:(i + 1) * nz, :] = local[i * nz:(i + 1) * nz] + (2.0 + w)

    def prepare(v, cs):
        for h in range(2):
            r = nz + h * half
            v[0, r:r + half, cs] = jnp.dot(shifts[1], v[n, r:r + half, cs], preferred_element_type=F32).astype(BF16)
            v[n + 1, r:r + half, cs] = jnp.dot(shifts[2], v[1, r:r + half, cs], preferred_element_type=F32).astype(BF16)

        @pl.loop(0, n, unroll=4)
        def _(p):
            CO[p] = jnp.dot(W[p], v[p + 1, nz:nz + plane, cs], preferred_element_type=F32)

        @pl.loop(0, n)
        def _(p):
            after = lax.rem(p + 1, n)
            energy = widen(BB[p, 2 * atoms:3 * atoms, 0:LANES], chunk)
            rest = energy * (CO[p, 0:atoms, :] + CO[after, atoms:2 * atoms, :])
            for term in range(3):
                part = rest.astype(BF16)
                rest = rest - part.astype(F32)
                r = term * 2 * atoms
                SP[p, r:r + atoms, :] = part
                SP[after, r + atoms:r + 2 * atoms, :] = part

    def operate(v, cs, finish):
        prepare(v, cs)

        @pl.loop(0, n)
        def _(p):
            for h in range(2):
                base = nz + h * half
                ACC[h] = (
                    jnp.dot(shifts[0], v[p + 1, base:base + half, cs], preferred_element_type=F32)
                    + jnp.dot(G[p, h * half:(h + 1) * half, :], SP[p], preferred_element_type=F32))
            inner = None
            centre = v[p + 1, nz:2 * nz, cs].astype(F32)
            for i in range(nr):
                ri = nr + i
                r = nz + i * nz
                q = i * nz - (half if i * nz >= half else 0)
                outer = v[p + 1, r + nz:r + 2 * nz, cs].astype(F32) if i < nr - 1 else None
                sides = v[p + 2, r:r + nz, cs].astype(F32) + v[p, r:r + nz, cs].astype(F32)
                local = widen(D[p, r - nz:r, :], chunk)
                value = (
                    ACC[i * nz // half, q:q + nz, :]
                    + (-0.5 * (nr / ri) ** 2) * sides
                    + local * centre)
                if outer is not None:
                    value = value + (-0.5 * (1.0 + 1.0 / (2.0 * ri))) * outer
                if inner is not None:
                    value = value + (-0.5 * (1.0 - 1.0 / (2.0 * ri))) * inner
                finish(p, r, centre, value)
                inner, centre = centre, outer

    def stage_first(c):
        cs = slice(c * chunk, (c + 1) * chunk)

        def finish(p, r, centre, value):
            A[p + 1, r:r + nz, :] = ((value - CENTER * centre) * (1.0 / HALF_SPAN)).astype(BF16)

        operate(O, cs, finish)

    def stage_filtered(c):
        cs = slice(c * chunk, (c + 1) * chunk)

        def finish(p, r, centre, value):
            start = O[p + 1, r:r + nz, cs].astype(F32)
            F[p + 1, r:r + nz, cs] = (
                (value - CENTER * centre) * (2.0 / HALF_SPAN) - start).astype(BF16)

        operate(A, slice(0, chunk), finish)

    def stage_image(c):
        cs = slice(c * chunk, (c + 1) * chunk)

        def finish(p, r, centre, value):
            I[p, r - nz:r, cs] = value.astype(BF16)

        operate(F, cs, finish)

    part = n // 2

    def panel_at(j, side, which):
        lane = pl.multiple_of((j + side * pieces) * LANES, LANES)
        return PB.at[pl.ds(which * part, part), :, pl.ds(lane, LANES)]

    def panel_out(j, d):
        to = lax.rem(b + d, nb)
        which = lax.rem(to, 2)
        return remote(F.at[pl.ds(1 + which * part, part), pl.ds(nz, plane), pl.ds(j * LANES, LANES)],
                      panel_at(j, x, which), ps.at[0, j, d], pr.at[0, j], band=to)

    def panel_cross(j, side):
        return remote(panel_at(j, side, core), panel_at(j, side, core), ps.at[1, j, 0], pr.at[1, j], sector=partner)

    def panel_pair(j, side, which, own):
        k = 2 if own else 3
        return remote(panel_at(j, side, which), panel_at(j, side, which), ps.at[k, j, 0], pr.at[k, j], band=sibling)

    def when_own(f):
        if both:
            f()
        else:
            pl.when(x == 0)(f)

    def when_other(f):
        if both:
            f()
        else:
            pl.when(x == 1)(f)

    def panel_one(j):
        def go():
            @pl.when(b == owner)
            def _():
                for d in range(1, nb):
                    panel_out(j, d).start()
                lane = pl.multiple_of((j + x * pieces) * LANES, LANES)

                @pl.loop(0, part)
                def _(p):
                    PB[core * part + p, :, pl.ds(lane, LANES)] = (
                        F[1 + core * part + p, nz:nz + plane, j * LANES:(j + 1) * LANES])
        when_own(go)

    def panel_two(j):
        def go():
            @pl.when(b != owner)
            def _():
                remote(panel_at(j, x, core), panel_at(j, x, core), ps.at[0, j, 0], pr.at[0, j], band=sibling).wait_recv()
            panel_cross(j, x).start()
            panel_pair(j, x, core, True).start()
        when_own(go)

    def panel_three(j):
        def go():
            panel_cross(j, 1 - x).wait_recv()
            panel_pair(j, 1 - x, core, False).start()
        when_other(go)

    def panel_ready():
        for j in range(pieces):
            when_own(lambda: panel_pair(j, x, 1 - core, True).wait_recv())
            when_other(lambda: panel_pair(j, 1 - x, 1 - core, False).wait_recv())

        @pl.loop(0, n)
        def _(p):
            PT[p] = PB[p].T

    def panel_done():
        for j in range(pieces):
            def own():
                @pl.when(b == owner)
                def _():
                    for d in range(1, nb):
                        panel_out(j, d).wait_send()
                panel_cross(j, x).wait_send()
                panel_pair(j, x, core, True).wait_send()
            when_own(own)
            when_other(lambda: panel_pair(j, 1 - x, core, False).wait_send())

    scale = 1.0 / (plane * n)

    def result_copies(g):
        theirs = pl.ds(pl.multiple_of((1 - x) * rows, 8), rows)
        return (remote(PH.at[g, theirs], RH.at[g], os.at[0, g], orr.at[0, g], sector=partner),
                remote(PG.at[g, theirs], RG.at[g], os.at[1, g], orr.at[1, g], sector=partner))

    def project(g):
        cs = slice(g * batch, (g + 1) * batch)
        PG[g] = jnp.dot(PT[0], F[1, nz:nz + plane, cs], preferred_element_type=F32)
        PH[g] = jnp.dot(PT[0], I[0, :, cs], preferred_element_type=F32)

        @pl.loop(1, n)
        def _(p):
            PG[g] += jnp.dot(PT[p], F[p + 1, nz:nz + plane, cs], preferred_element_type=F32)
            PH[g] += jnp.dot(PT[p], I[p, :, cs], preferred_element_type=F32)

        for copy in result_copies(g):
            copy.start()
        ours = pl.ds(pl.multiple_of(x * rows, 8), rows)
        for q in range(batch // LANES):
            place = pl.ds(source_lane(g * (batch // LANES) + q, x), LANES)
            lanes = slice(q * LANES, (q + 1) * LANES)
            gram[:, place] = PG[g, ours, lanes] * scale
            ham[:, place] = PH[g, ours, lanes] * scale

    def collect(g):
        for copy in result_copies(g):
            copy.wait_recv()
        for q in range(batch // LANES):
            place = pl.ds(source_lane(g * (batch // LANES) + q, 1 - x), LANES)
            lanes = slice(q * LANES, (q + 1) * LANES)
            gram[:, place] = RG[g, :, lanes] * scale
            ham[:, place] = RH[g, :, lanes] * scale

    span = levels
    last_slot = SKEW * (chunks - 1) + span - 1
    work = {}

    def put(t, f, *args):
        work.setdefault(t, []).append(functools.partial(f, *args))

    put(span - 1, setup)
    for c in range(chunks):
        t = SKEW * c + span - 1
        put(t, stage_first, c)
        put(t, stage_filtered, c)
        for j in range(pieces):
            if ((j + 1) * LANES - 1) // chunk == c:
                put(t, panel_one, j)
                put(t + 1, panel_two, j)
                put(t + 2, panel_three, j)
    for c in range(chunks):
        put(SKEW * c + span, stage_image, c)
    for g in range(batches):
        need = ((g + 1) * batch - 1) // chunk
        t = SKEW * need + span + 1
        if g == 0:
            piece_slot = SKEW * ((pieces * LANES - 1) // chunk) + span + 2
            t = max(t, piece_slot)
            put(t, panel_ready)
            first_project = t
        put(max(t, first_project), project, g)

    for t in range(last_slot + 1):
        if t == 0:
            bundle_cross_wait()
        if 0 < t < levels:
            receives(bundle_hop, t - 1)
        if t < levels - 1:
            sends(bundle_hop, t, lambda copy: copy.start())
        for c in range(chunks):
            k = t - SKEW * c
            if 0 <= k < levels:
                if k == 0:
                    cross_wait(c)
                else:
                    receives(chunk_hop(c), k - 1)
                if k < levels - 1:
                    sends(chunk_hop(c), k, lambda copy: copy.start())
        for item in work.get(t, []):
            item()
    for t in sorted(work):
        if t > last_slot:
            for item in work[t]:
                item()
    for g in range(batches):
        collect(g)

    bundle_cross().wait_send()
    for c in range(chunks):
        cross(c).wait_send()
    for k in range(levels - 1):
        sends(bundle_hop, k, lambda copy: copy.wait_send())
        for c in range(chunks):
            sends(chunk_hop(c), k, lambda copy: copy.wait_send())
    panel_done()
    for g in range(batches):
        for copy in result_copies(g):
            copy.wait_send()


def shift_matrices(size, nz):
    row = jnp.arange(size)[:, None]
    col = jnp.arange(size)[None, :]
    same = row // nz == col // nz
    gap = (col - row) % nz
    near = jnp.where(same & ((gap == 1) | (gap == nz - 1)), -0.5, 0.0)
    lower = jnp.where(same & (gap == nz - TWIST), 1.0, 0.0)
    upper = jnp.where(same & (gap == TWIST), 1.0, 0.0)
    return jnp.stack([near, lower, upper]).astype(BF16)


def on_device(n, nb, orbitals, potential, near_points, near_values, far_points, far_values, atom_energy):
    _, nr, nz, cols = orbitals.shape
    plane = nr * nz
    atoms = near_points.shape[0]
    near = build_dense(near_points, near_values, plane).astype(F32)
    far = build_dense(far_points, far_values, plane).astype(F32)
    energy = jnp.broadcast_to(atom_energy[:, None], (atoms, plane))
    local = jnp.broadcast_to(potential.reshape(1, plane), (8, plane))
    bund = jnp.concatenate([near, far, energy, local], axis=0)
    shifts = shift_matrices(plane // 2, nz)
    mine = cols // 2
    chunk = LANES
    batch = min(2 * LANES, mine)
    chunks, batches = mine // chunk, mine // batch
    rows = PANEL // n
    panel_dev = PANEL // nb
    pieces = max(panel_dev // LANES // 2, 1)
    hops = n // 2 - 1
    tall = plane + 2 * nz
    vmem = pl.BlockSpec(memory_space=pltpu.VMEM)
    dma = pltpu.SemaphoreType.DMA
    return pl.pallas_call(
        functools.partial(kernel, n, nb, nr, nz, atoms, chunk, batch),
        out_shape=(jax.ShapeDtypeStruct((rows, cols), F32),) * 2,
        in_specs=[vmem] * 3,
        out_specs=(vmem,) * 2,
        scratch_shapes=[
            pltpu.VMEM((n + 2, tall, mine), BF16),
            pltpu.VMEM((n + 2, tall, chunk), BF16),
            pltpu.VMEM((n + 2, tall, mine), BF16),
            pltpu.VMEM((n, plane, mine), BF16),
            pltpu.VMEM((n,) + bund.shape, F32),
            pltpu.VMEM((n, 2 * atoms, plane), BF16),
            pltpu.VMEM((n, plane, LANES), BF16),
            pltpu.VMEM((n, plane, LANES), F32),
            pltpu.VMEM((n, 2 * atoms, chunk), F32),
            pltpu.VMEM((n, LANES, chunk), BF16),
            pltpu.VMEM((2, plane // 2, chunk), F32),
            pltpu.VMEM((n, plane, panel_dev), BF16),
            pltpu.VMEM((n, panel_dev, plane), BF16),
            pltpu.VMEM((batches, panel_dev, batch), F32),
            pltpu.VMEM((batches, panel_dev, batch), F32),
            pltpu.VMEM((batches, rows, batch), F32),
            pltpu.VMEM((batches, rows, batch), F32),
            dma((chunks,)),
            dma((chunks,)),
            dma((2, chunks, hops)),
            dma((2, chunks, hops)),
            dma,
            dma,
            dma((2, hops)),
            dma((2, hops)),
            dma((4, pieces, nb)),
            dma((4, pieces)),
            dma((2, batches)),
            dma((2, batches)),
        ],
        compiler_params=pltpu.CompilerParams(
            collective_id=0, has_side_effects=True, vmem_limit_bytes=60 * 2 ** 20
        ),
    )(orbitals.reshape(plane, cols), bund, shifts)


def solution(mesh):
    n, nb = mesh.shape["sector"], mesh.shape["band"]
    return jax.shard_map(
        functools.partial(on_device, n, nb),
        mesh=mesh,
        in_specs=(
            P("sector", None, None, "band"),
            P("sector", None, None),
            P("sector", None),
            P("sector", None),
            P("sector", None),
            P("sector", None),
            P("sector"),
        ),
        out_specs=(P("sector", "band"), P("sector", "band")),
        check_vma=False,
    )
```

time: 154 us -> 148 us (0.961); the launches traced: 153 us -> 145 us
  Pallas kernels: 142 us -> 134 us
    pallas_call x1, Pallas kernels: 142 us -> 134 us  [on_device(): pl.pallas_call(functools.partial(kernel, n, nb, nr, nz, atoms, chunk, bat...]
where the time goes in v2:
time: 148 us; the launch traced here: 145 us
  Pallas kernels  134 us (91%)
  other arithmetic  5.2 us (4%)
  local copies, waits for them, and re-layouts  4.96 us (3%)
    pallas_call x1, Pallas kernels, on_device(): pl.pallas_call(functools.partial(kernel, n, nb, nr, nz, atoms, chunk, bat...  134 us
    unnamed x5, local copies, waits for them, and re-layouts  4.14 us

profile of v2, /device:TPU:0, one launch (start us, length us, event | category | flops | bytes accessed | tf_op | source)
XLA Modules:
  0.0 145.0 jit_solution(13843765915596526061)
XLA Ops:
  0.6 0.7 pad.5.clone
  1.4 0.7 convert_element_type.21
  2.1 1.1 select_reduce_fusion
  3.2 0.7 convert_element_type.24
  3.9 0.9 select_reduce_fusion.1
  4.8 0.8 copy.10
  5.6 0.1 broadcast_in_dim.36
  5.7 0.7 pad_maximum_fusion.1.bund
  6.4 0.3 select_convert_fusion.2
  6.7 0.8 pad_maximum_fusion.shifts
  7.5 134.1 %shard_map.86 = (f32[256,1024]{1,0:T(8,128)}, f32[256,1024]{1,0:T(8,128)}) custom-call(bf16[512,1024]{1,0:T(8,128)(2,1)} %bitcast.1, f32[56,512]{1,0:T(8,128)} %pad_maximum_fusion.1.bund, bf16[3,256,256]{2,1,0:T(8,128)(2,1)} %pad_maximum_fusion.shifts), custom_call_target="tpu_custom_call" | custom-call | tf_op jit(solution)/shard_map/pallas_call | solution.py:457
  141.6 0.0 copy-start
  141.6 2.4 %copy.13 = f32[256,1024]{1,0:T(8,128)} copy(f32[256,1024]{1,0:T(8,128)} %get-tuple-element.7) | data formatting | bytes 2097152
  144.0 0.0 copy-done
  144.0 1.0 copy.14
  (4 shorter events, 0.0 us)
Async XLA Ops:
  141.6 2.4 %copy-start = (f32[256,1024]{1,0:T(8,128)S(1)}, f32[256,1024]{1,0:T(8,128)}, u32[]{:S(2)}) copy-start(f32[256,1024]{1,0:T(8,128)} %get-tuple-element.8) | copy-start | bytes 3145732

commit v3 on v2

--- a/solution.py
+++ b/solution.py
@@ -16,7 +16,7 @@
 CENTER = 6.0
 HALF_SPAN = 3.0
 LANES = 128
-SKEW = 2
+SKEW = 1
 
 
 def build_dense(points, values, width):

time: 148 us -> 157 us (1.061)
  the two profiles are of different devices: /device:TPU:0 before, /device:TPU:27 now
where the time goes in v3:
time: 157 us
  Pallas kernels  146 us (93%)
  other arithmetic  5.2 us (3%)
  local copies, waits for them, and re-layouts  4.96 us (3%)
    pallas_call x1, Pallas kernels, on_device(): pl.pallas_call(functools.partial(kernel, n, nb, nr, nz, atoms, chunk, bat...  146 us
    unnamed x5, local copies, waits for them, and re-layouts  4.14 us

profile of v3, /device:TPU:27, one launch (start us, length us, event | category | flops | bytes accessed | tf_op | source)
XLA Modules:
  0.0 157.0 jit_solution(848866583431883969)
XLA Ops:
  0.6 0.7 pad.5.clone
  1.4 0.7 convert_element_type.21
  2.1 1.1 select_reduce_fusion
  3.2 0.7 convert_element_type.24
  3.9 0.9 select_reduce_fusion.1
  4.8 0.8 copy.10
  5.6 0.1 broadcast_in_dim.36
  5.7 0.7 pad_maximum_fusion.1.bund
  6.4 0.3 select_convert_fusion.2
  6.7 0.8 pad_maximum_fusion.shifts
  7.5 146.2 %shard_map.86 = (f32[256,1024]{1,0:T(8,128)}, f32[256,1024]{1,0:T(8,128)}) custom-call(bf16[512,1024]{1,0:T(8,128)(2,1)} %bitcast.1, f32[56,512]{1,0:T(8,128)} %pad_maximum_fusion.1.bund, bf16[3,256,256]{2,1,0:T(8,128)(2,1)} %pad_maximum_fusion.shifts), custom_call_target="tpu_custom_call" | custom-call | tf_op jit(solution)/shard_map/pallas_call | solution.py:457
  153.7 0.0 copy-start
  153.7 2.4 %copy.13 = f32[256,1024]{1,0:T(8,128)} copy(f32[256,1024]{1,0:T(8,128)} %get-tuple-element.7) | data formatting | bytes 2097152
  156.1 0.0 copy-done
  156.1 1.0 copy.14
  (4 shorter events, 0.0 us)
Async XLA Ops:
  153.7 2.4 %copy-start = (f32[256,1024]{1,0:T(8,128)S(1)}, f32[256,1024]{1,0:T(8,128)}, u32[]{:S(2)}) copy-start(f32[256,1024]{1,0:T(8,128)} %get-tuple-element.8) | copy-start | bytes 3145732
